TPU v7x, 32 devices: a whole 2x2x4 slice. The times are simulated.
32 devices in a mesh: dp: 4 (over x, core), seq: 8 (over z, y).
Axes of the slice: x: 2, y: 2, z: 4, core: 2. Of those that a mesh axis runs over, the one named last changes fastest.
Arguments:
- hidden: bfloat16 [4, 1024, 2048], P('dp', 'seq'), may hold values from -6 to 6
- tokens: int32 [4, 1024], P('dp', 'seq'), may hold values from 0 to 4
- embedding: float32 [5, 2048], replicated, may hold values from -6 to 6
- weight: bfloat16 [2048, 1024], P('dp'), may hold values from -0.125 to 0.125
- kernel: float32 [7, 1024], replicated, may hold values from -2.4 to 2.4
- cotangent: bfloat16 [4, 1024, 1024], P('dp', 'seq'), may hold values from -6 to 6
Outputs:
- block_result: bfloat16 [4, 1024, 1024], P('dp', 'seq')
- grad_hidden: bfloat16 [4, 1024, 2048], P('dp', 'seq')
- grad_weight: float32 [2048, 1024], P('dp')
- grad_kernel: float32 [7, 1024], replicated
- grad_embedding: float32 [5, 2048], replicated
All inputs are finite; a program needn't handle non-finite values.
Results may differ from a plain program's by a relative error of at most 0.0095.
Values may be sent and summed in bfloat16 or wider, within the bound.
A program may use at most 64 MiB of HBM per device.

v0:
```python
import functools
import math

import jax
import jax.numpy as jnp
from jax import lax
from jax.experimental import pallas as pl
from jax.experimental.pallas import tpu as pltpu
from jax.sharding import PartitionSpec as P

MESH = pl.DeviceIdType.MESH
F32 = jnp.float32
BF16 = jnp.bfloat16
EDGE = 16
CHUNKS = 4
PIECES = 4
LANES = 256


def level_plan(rows, bits):
    groups = [[0], [1, 2]] + [[b] for b in range(3, bits)] if bits >= 3 else [[b] for b in range(bits)]
    levels = []
    for group in groups:
        ways = 1 << len(group)
        split = rows % (16 * ways) == 0
        if split:
            rows //= ways
            levels.append((group, rows, True))
        else:
            levels += [([b], rows, False) for b in group]
    return levels


def body(
    seq_count, bits, factor,
    hid_in, tok_in, emb_in, w_in, ker_in, cot_in,
    block_ref, hout_ref, gw_ref, kernel_ref, table_ref,
    hid_ref, tok_ref, emb_ref, ker_ref, cot_ref,
    wg, sx, hx, ux, hu, s2t, s2tp, val, gmix, sigs, outs, routs, gv, gvp, fwd_back, rev_back,
    acc, core_send, core_recv, seq_send, seq_recv, gathered,
    small, small_recv, small_ref,
    in_sems, w_ss, w_rs, h_ss, h_rs, r_ss, r_rs, s_ss, s_rs,
):
    rows = hid_ref.shape[0]
    depth, units = w_in.shape
    width = hid_ref.shape[1]
    taps = ker_ref.shape[0]
    reach = (taps - 1) // 2
    vocab = emb_ref.shape[0]
    total = rows + 2 * EDGE
    dp = lax.axis_index("dp")
    seq = lax.axis_index("seq")
    xi, ci = dp // 2, dp % 2
    loads = [
        pltpu.make_async_copy(src, dst, in_sems.at[n])
        for n, (src, dst) in enumerate(
            [(w_in, wg.at[dp]), (cot_in, cot_ref), (hid_in, hid_ref), (tok_in, tok_ref), (emb_in, emb_ref), (ker_in, ker_ref)]
        )
    ]
    for copy in loads:
        copy.start()
    core_id = (dp + 1 - 2 * ci, seq)
    x_id = (dp + 2 - 4 * xi, seq)
    bit_vals = [(seq // (1 << b)) % 2 for b in range(bits)]
    bit_ids = [(dp, seq + (1 - 2 * bit_vals[b]) * (1 << b)) for b in range(bits)]
    left_id = (dp, (seq + seq_count - 1) % seq_count)
    right_id = (dp, (seq + 1) % seq_count)

    levels = level_plan(depth, bits)
    exchanges = [(n, d) for n, (group, _, _) in enumerate(levels) for d in range(1, 1 << len(group))]

    def peer_id(n, d):
        place = seq
        for at_bit, b in enumerate(levels[n][0]):
            if (d >> at_bit) & 1:
                place = place + (1 - 2 * bit_vals[b]) * (1 << b)
        return (dp, place)

    def digit(n, d):
        value = 0
        for at_bit, b in enumerate(levels[n][0]):
            bit = bit_vals[b]
            value = value + (1 - bit if (d >> at_bit) & 1 else bit) * (1 << at_bit)
        return value

    partners = [core_id, x_id] + [peer_id(n, d) for n, d in exchanges] + [left_id, right_id]
    barrier = pltpu.get_barrier_semaphore()
    for partner in partners:
        pl.semaphore_signal(barrier, inc=1, device_id=partner, device_id_type=MESH)
    pl.semaphore_wait(barrier, len(partners))

    def remote(src, dst, ss, rs, who):
        return pltpu.make_async_remote_copy(
            src_ref=src, dst_ref=dst, send_sem=ss, recv_sem=rs, device_id=who, device_id_type=MESH
        )

    yi = bit_vals[0]
    y_id = bit_ids[0]
    dpx = dp + 2 - 4 * xi
    half = depth // 2
    piece = half // PIECES

    def span(side, p):
        return pl.ds(pl.multiple_of(side * half + p * piece, 16), piece)

    sends = []
    over_x = [
        remote(wg.at[dp, span(yi, p)], wg.at[dp, span(yi, p)], w_ss.at[p], w_rs.at[p], x_id)
        for p in range(PIECES)
    ]
    loads[0].wait()
    for copy in over_x[:2]:
        copy.start()
    loads[1].wait()
    own = remote(wg.at[dp], wg.at[dp], w_ss.at[4 * PIECES], w_rs.at[4 * PIECES], core_id)
    own.start()
    sends += over_x + [own]
    halo_u = [
        remote(cot_ref.at[pl.ds(rows - EDGE, EDGE)], hu.at[0], h_ss.at[0], h_rs.at[0], right_id),
        remote(cot_ref.at[pl.ds(0, EDGE)], hu.at[1], h_ss.at[1], h_rs.at[1], left_id),
    ]
    for copy in halo_u:
        copy.start()

    tile = LANES
    for copy in loads[2:]:
        copy.wait()
    tok = jnp.broadcast_to(tok_ref[...], (rows, rows)).astype(F32).T
    tok = jnp.concatenate([tok] * (tile // rows), axis=1) if tile > rows else tok[:, :tile]

    def stream_tile(i, carry):
        cols = pl.ds(pl.multiple_of(i * tile, tile), tile)
        looked = jnp.zeros((rows, tile), F32)
        for k in range(vocab):
            looked = looked + jnp.where(tok == float(k), emb_ref[pl.ds(k, 1), cols], 0.0)
        sx[0, pl.ds(EDGE, rows), cols] = (hid_ref[:, cols].astype(F32) + looked).astype(BF16)
        return carry

    lax.fori_loop(0, width // tile, stream_tile, 0)
    halo_s = [
        remote(sx.at[0, pl.ds(rows, EDGE)], hx.at[0], h_ss.at[2], h_rs.at[2], right_id),
        remote(sx.at[0, pl.ds(EDGE, EDGE)], hx.at[1], h_ss.at[3], h_rs.at[3], left_id),
    ]
    for copy in halo_s:
        copy.start()
    sends += halo_u + halo_s

    over_y, over_core = [], []

    def arrived(p):
        over_x[p].wait_recv()
        if p + 2 < PIECES:
            over_x[p + 2].start()
        part = wg.at[dpx, span(yi, p)]
        over_y.append(remote(part, part, w_ss.at[PIECES + p], w_rs.at[PIECES + p], y_id))
        over_core.append(remote(part, part, w_ss.at[2 * PIECES + p], w_rs.at[2 * PIECES + p], core_id))
        over_y[p].start()
        over_core[p].start()

    has_left = (seq > 0).astype(F32)
    has_right = (seq < seq_count - 1).astype(F32)
    ux[0, pl.ds(EDGE, rows), :] = cot_ref[...]
    arrived(0)
    for copy in halo_u + halo_s:
        copy.wait_recv()
    sx[0, pl.ds(0, EDGE), :] = (hx[0].astype(F32) * has_left).astype(BF16)
    sx[0, pl.ds(rows + EDGE, EDGE), :] = (hx[1].astype(F32) * has_right).astype(BF16)
    ux[0, pl.ds(0, EDGE), :] = (hu[0].astype(F32) * has_left).astype(BF16)
    ux[0, pl.ds(rows + EDGE, EDGE), :] = (hu[1].astype(F32) * has_right).astype(BF16)

    arrived(1)

    flip = (
        lax.broadcasted_iota(jnp.int32, (tile, tile), 0)
        + lax.broadcasted_iota(jnp.int32, (tile, tile), 1)
        == tile - 1
    ).astype(F32).astype(BF16)

    def mirrored(block):
        return jnp.dot(block, flip, preferred_element_type=F32)

    def reverse_stream(i, carry):
        cols = pl.ds(pl.multiple_of(i * tile, tile), tile)
        back = pl.ds(pl.multiple_of(width - tile - i * tile, tile), tile)
        sx[1, :, back] = mirrored(sx[0, :, cols]).astype(BF16)
        return carry

    lax.fori_loop(0, width // tile, reverse_stream, 0)

    def reverse_up(i, carry):
        cols = pl.ds(pl.multiple_of(i * tile, tile), tile)
        back = pl.ds(pl.multiple_of(units - tile - i * tile, tile), tile)
        ux[1, :, back] = mirrored(ux[0, :, cols]).astype(BF16)
        return carry

    lax.fori_loop(0, units // tile, reverse_up, 0)

    def project(block, first):
        depth_cols = pl.ds(pl.multiple_of(block * depth, depth), depth)

        def project_tile(i, carry):
            cols = pl.ds(pl.multiple_of(i * tile, tile), tile)
            for s in range(2):
                part = jnp.dot(sx[s, :, depth_cols], wg[block, :, cols], preferred_element_type=F32)
                if first:
                    val[s, :, cols] = part
                else:
                    val[s, :, cols] += part
            return carry

        lax.fori_loop(0, units // tile, project_tile, 0)

    project(dp, True)

    arrived(2)
    own.wait_recv()
    project(dp + 1 - 2 * ci, False)

    def transpose_tile(i, carry):
        cols = pl.ds(pl.multiple_of(i * tile, tile), tile)
        for s in range(2):
            s2t[cols, pl.ds(s * rows, rows)] = sx[s, pl.ds(EDGE, rows), cols].T
        return carry

    lax.fori_loop(0, width // tile, transpose_tile, 0)
    for p in range(3, PIECES):
        arrived(p)
    stream_copy = remote(
        s2t.at[pl.ds(pl.multiple_of((1 - xi) * 2 * depth, depth), 2 * depth)], s2tp, h_ss.at[4], h_rs.at[4], x_id
    )
    stream_copy.start()
    sends.append(stream_copy)
    over_core2 = []
    for p in range(PIECES):
        over_y[p].wait_recv()
        other = 1 - yi
        over_core2.append(
            remote(wg.at[dpx, span(other, p)], wg.at[dpx, span(other, p)], w_ss.at[3 * PIECES + p], w_rs.at[3 * PIECES + p], core_id)
        )
        over_core2[p].start()
    sends += over_y + over_core + over_core2
    for p in range(PIECES):
        over_core[p].wait_recv()
        over_core2[p].wait_recv()

    ew = 128
    cw = units // CHUNKS
    lo = EDGE - 8

    rt = 32

    def strand_tile(i, carry):
        cols = pl.ds(pl.multiple_of(i * ew, ew), ew)
        inner = pl.ds(pl.multiple_of((i % (cw // ew)) * ew, ew), ew)
        tap_rows = [ker_ref[pl.ds(k, 1), cols] for k in range(taps)]
        tap_sums = [jnp.zeros((8, ew), F32)] * taps
        for s in range(2):
            for r in range(0, rows + 16, rt // 2):
                at = pl.ds(lo + r, rt // 2)
                part = val[s, at, cols].astype(BF16).astype(F32)
                val[s, at, cols] = part
                logistic = jax.nn.sigmoid(part)
                gate = part * logistic
                sigs[s, pl.ds(r, rt // 2), :] = logistic
                gmix[s, pl.ds(r, rt // 2), :] = ux[s, at, cols].astype(F32) * gate
            for r in range(0, rows, rt):
                lin = val[s, pl.ds(EDGE + r, rt), cols]
                sig = sigs[s, pl.ds(8 + r, rt), :]
                up = ux[s, pl.ds(EDGE + r, rt), cols].astype(F32)
                mine = gmix[s, pl.ds(8 + r, rt), :]
                mixing = jnp.zeros((rt, ew), F32)
                spread = jnp.zeros((rt, ew), F32)
                for m in range(taps):
                    k = m if s == 0 else taps - 1 - m
                    row = tap_rows[k]
                    shifted = val[s, pl.ds(EDGE + r + m - reach, rt), cols]
                    mixing = mixing + row * shifted
                    product_sum = mine * shifted
                    for q in range(0, rt, 8):
                        tap_sums[k] = tap_sums[k] + product_sum[q : q + 8]
                    spread = spread + row * gmix[s, pl.ds(8 + r + reach - m, rt), :]
                strand_out = mixing * (lin * sig)
                if s == 0:
                    outs[pl.ds(r, rt), cols] = strand_out
                else:
                    routs[pl.ds(r, rt), cols] = strand_out.astype(BF16)
                grad = up * mixing * sig * (1.0 + lin * (1.0 - sig)) + spread
                gv[i // (cw // ew), pl.ds(s * rows + r, rt), inner] = grad.astype(BF16)
        tap_sums = [jnp.sum(value, axis=0, keepdims=True) for value in tap_sums]
        small_cols = pl.ds(pl.multiple_of((i % (units // 2 // ew)) * ew, ew), ew)
        pad = [jnp.zeros((1, ew), F32)] * (8 - taps)
        small[i // (units // 2 // ew), pl.ds(0, 8), small_cols] = jnp.concatenate(tap_sums + pad, axis=0)
        return carry

    def elementwise(j):
        cols = pl.ds(j * cw, cw)
        for block in (dpx, dpx + 1 - 2 * ci):
            depth_cols = pl.ds(pl.multiple_of(block * depth, depth), depth)
            for s in range(2):
                val[s, :, cols] += jnp.dot(sx[s, :, depth_cols], wg[block, :, cols], preferred_element_type=F32)
        lax.fori_loop(j * (cw // ew), (j + 1) * (cw // ew), strand_tile, 0)
        grad_copy(j).start()

    def grad_copy(j):
        return remote(gv.at[j], gvp.at[j], r_ss.at[j, 1], r_rs.at[j, 1], x_id)

    def core_copy(j):
        return remote(core_send.at[j], core_recv.at[j], r_ss.at[j, 0], r_rs.at[j, 0], core_id)

    def product(j):
        grad_copy(j).wait_recv()
        if j == 0:
            stream_copy.wait_recv()
        for side in range(2):
            block = 1 - ci if side == 0 else ci
            mine = pl.ds(pl.multiple_of((2 * xi + block) * depth, depth), depth)
            theirs = pl.ds(pl.multiple_of(block * depth, depth), depth)
            result = jnp.dot(s2t[mine, :], gv[j], preferred_element_type=F32)
            result = result + jnp.dot(s2tp[theirs, :], gvp[j], preferred_element_type=F32)
            if side == 0:
                core_send[j] = result.astype(BF16)
                core_copy(j).start()
            else:
                acc[j] = result

    def after_core(j):
        core_copy(j).wait_recv()
        acc[j] += core_recv[j].astype(F32)
        rs_start(j, 0)

    bases = [0]
    for n, (_, size, split) in enumerate(levels):
        bases.append(bases[-1] + digit(n, 0) * size if split else bases[-1])

    def rows_at(n, d):
        size, split = levels[n][1:]
        base = bases[n] + digit(n, d) * size if split else bases[n]
        return pl.ds(pl.multiple_of(base, 16), size)

    slots, at = {}, 0
    for n, d in exchanges:
        slots[n, d] = at
        at += levels[n][1]
    number = {pair: k for k, pair in enumerate(exchanges)}
    ways = [[d for m, d in exchanges if m == n] for n in range(len(levels))]

    def rs_copy(j, n, d):
        where = pl.ds(slots[n, d], levels[n][1])
        sem = 2 + number[n, d]
        return remote(seq_send.at[j, where], seq_recv.at[j, where], r_ss.at[j, sem], r_rs.at[j, sem], peer_id(n, d))

    def rs_start(j, n):
        for d in ways[n]:
            seq_send[j, pl.ds(slots[n, d], levels[n][1]), :] = acc[j, rows_at(n, d), :].astype(BF16)
            rs_copy(j, n, d).start()

    def rs_finish(j, n):
        for d in ways[n]:
            rs_copy(j, n, d).wait_recv()
        total_rows = acc[j, rows_at(n, 0), :]
        for d in ways[n]:
            total_rows = total_rows + seq_recv[j, pl.ds(slots[n, d], levels[n][1]), :].astype(F32)
        acc[j, rows_at(n, 0), :] = total_rows

    gathers = [n for n in reversed(range(len(levels))) if levels[n][2]]

    def ag_copy(j, n, d):
        size = levels[n][1]
        ref = gathered.at[j, pl.ds(pl.multiple_of(bases[n + 1], 16), size)]
        sem = 2 + len(exchanges) + number[n, d]
        return remote(ref, ref, r_ss.at[j, sem], r_rs.at[j, sem], peer_id(n, d))

    def ag_start(j, n):
        for d in ways[n]:
            ag_copy(j, n, d).start()

    def stages(j):
        def after_rs(n):
            rs_finish(j, n)
            if n + 1 < len(levels):
                rs_start(j, n + 1)
            else:
                last = rows_at(n, 0)
                gathered[j, last, :] = acc[j, last, :].astype(BF16)
                ag_start(j, gathers[0])

        def after_ag(k):
            for d in ways[gathers[k]]:
                ag_copy(j, gathers[k], d).wait_recv()
            if k + 1 < len(gathers):
                ag_start(j, gathers[k + 1])
            else:
                gw_ref[:, pl.ds(j * cw, cw)] = gathered[j]

        steps = [functools.partial(stage, j) for stage in (elementwise, product, after_core)]
        steps += [functools.partial(after_rs, b) for b in range(len(levels))]
        steps += [functools.partial(after_ag, n) for n in range(len(gathers))]
        return steps

    def back_tile(i, carry):
        b = i // (depth // tile)
        r = pl.ds(pl.multiple_of((i % (depth // tile)) * tile, tile), tile)
        cols = pl.ds(pl.multiple_of(i * tile, tile), tile)
        mirror = pl.ds(pl.multiple_of(width - tile - i * tile, tile), tile)
        part = jnp.zeros((2 * rows, tile), F32)
        for j in range(CHUNKS):
            part = part + lax.dot_general(
                gv[j], wg[b, r, pl.ds(j * cw, cw)], (((1,), (1,)), ((), ())), preferred_element_type=F32
            )
        fwd_back[:, cols] = part[:rows]
        rev_back[:, mirror] = mirrored(part[rows:].astype(BF16))
        return carry

    one_hot = (
        lax.broadcasted_iota(jnp.int32, (8, rows), 0) == tok_ref[...]
    ).astype(F32).astype(BF16)

    def input_tile(i, carry):
        cols = pl.ds(pl.multiple_of(i * tile, tile), tile)
        grad = fwd_back[:, cols] + rev_back[:, cols]
        top = grad.astype(BF16)
        hout_ref[:, cols] = top
        left = grad - top.astype(F32)
        mid = left.astype(BF16)
        low = (left - mid.astype(F32)).astype(BF16)
        table = jnp.dot(one_hot, top, preferred_element_type=F32)
        table = table + jnp.dot(one_hot, mid, preferred_element_type=F32)
        table = table + jnp.dot(one_hot, low, preferred_element_type=F32)
        per = units // 2 // tile
        where = pl.ds(pl.multiple_of((i % per) * tile, tile), tile)
        at_rows = pl.ds(pl.multiple_of(8 + 8 * ((i // per) % 2), 8), 8)
        small[i // (2 * per), at_rows, where] = table
        return carry


    small_ids = [core_id, x_id] + bit_ids

    def small_copy(n):
        src = small.at[1 - ci] if n == 0 else small.at[2 + (n - 1) % 2]
        return remote(src, small_recv.at[n], s_ss.at[n], s_rs.at[n], small_ids[n])

    def small_last():
        return remote(small_ref.at[ci], small_ref.at[ci], s_ss.at[bits + 2], s_rs.at[bits + 2], core_id)

    def small_step(n):
        small_copy(n).wait_recv()
        base = small[ci] if n == 0 else small[2 + (n - 1) % 2]
        now = base + small_recv[n]
        if n < bits + 1:
            if n >= 2:
                small_copy(n - 1).wait_send()
            small[2 + n % 2] = now
            small_copy(n + 1).start()
        else:
            small_ref[ci] = now
            small_last().start()

    def result_tile(i, carry):
        cols = pl.ds(pl.multiple_of(i * tile, tile), tile)
        mirror = pl.ds(pl.multiple_of(units - tile - i * tile, tile), tile)
        block_ref[:, cols] = (outs[:, cols] + mirrored(routs[:, mirror])).astype(BF16)
        return carry

    tiles = width // tile

    def fill_back(part):
        lax.fori_loop(part * tiles // 4, (part + 1) * tiles // 4, back_tile, 0)

    def fill_input():
        lax.fori_loop(0, tiles, input_tile, 0)
        small_copy(0).start()

    def fill_result():
        lax.fori_loop(0, units // tile, result_tile, 0)
        small_step(0)

    fillers = [functools.partial(fill_back, part) for part in range(4)] + [fill_input, fill_result]
    fillers += [functools.partial(small_step, n) for n in range(1, bits + 2)]

    plans = [stages(j) for j in range(CHUNKS)]
    length = len(plans[0])
    for wave in range(length + CHUNKS - 1):
        if wave < CHUNKS:
            plans[wave][0]()
        for j in range(CHUNKS):
            if 1 <= wave - j < length:
                plans[j][wave - j]()
                if wave >= CHUNKS and fillers:
                    fillers.pop(0)()
    for filler in fillers:
        filler()
    small_last().wait_recv()
    for h in range(2):
        kernel_ref[:, pl.ds(h * units // 2, units // 2)] = small_ref[h, :taps, :] * factor
        for q in range(2):
            columns = pl.ds((2 * h + q) * (units // 2), units // 2)
            table_ref[:, columns] = small_ref[h, 8 + 8 * q : 8 + 8 * q + vocab, :] * factor

    for copy in sends:
        copy.wait_send()
    for j in range(CHUNKS):
        core_copy(j).wait_send()
        grad_copy(j).wait_send()
        for n, d in exchanges:
            rs_copy(j, n, d).wait_send()
            if levels[n][2]:
                ag_copy(j, n, d).wait_send()
    small_copy(0).wait_send()
    small_copy(bits).wait_send()
    small_copy(bits + 1).wait_send()
    small_last().wait_send()


def finish(factor, b_in, h_in, g_in, k_in, t_in, b_out, h_out, g_out, k_out, t_out, narrow, wide, sems):
    copies = [
        pltpu.make_async_copy(src, dst, sems.at[n])
        for n, (src, dst) in enumerate([(h_in, h_out), (b_in, b_out), (k_in, k_out), (t_in, t_out)])
    ]
    step = g_in.shape[0] // 4
    parts = [pl.ds(q * step, step) for q in range(4)]
    fetches = [pltpu.make_async_copy(g_in.at[part], narrow.at[part], sems.at[8 + q]) for q, part in enumerate(parts)]
    for copy in fetches:
        copy.start()
    for copy in copies:
        copy.start()
    for q, part in enumerate(parts):
        fetches[q].wait()
        wide[part, :] = narrow[part, :].astype(F32) * factor
        copies.append(pltpu.make_async_copy(wide.at[part], g_out.at[part], sems.at[4 + q]))
        copies[-1].start()
    for copy in copies:
        copy.wait()


def local(seq_count, hidden, tokens, embedding, weight, kernel, cotangent):
    window, token_codes, upstream = hidden[0], tokens[0], cotangent[0]
    rows, width = window.shape
    depth, units = weight.shape
    blocks = width // depth
    taps, vocab = kernel.shape[0], embedding.shape[0]
    bits = seq_count.bit_length() - 1
    positions = hidden.shape[0] * rows * lax.axis_size("dp") * seq_count
    total = rows + 2 * EDGE
    cw = units // CHUNKS
    factor = 1.0 / math.sqrt(positions)
    levels = level_plan(depth, bits)
    stacked_rows = sum(size * ((1 << len(group)) - 1) for group, size, _ in levels)
    copies = sum((1 << len(group)) - 1 for group, _, _ in levels)
    vmem = pl.BlockSpec(memory_space=pltpu.VMEM)
    dma = pltpu.SemaphoreType.DMA
    block_result, grad_hidden, grad_weight, kernel_sum, table = pl.pallas_call(
        functools.partial(body, seq_count, bits, factor),
        out_shape=(
            jax.ShapeDtypeStruct((rows, units), BF16),
            jax.ShapeDtypeStruct((rows, width), BF16),
            jax.ShapeDtypeStruct((depth, units), BF16),
            jax.ShapeDtypeStruct((taps, units), F32),
            jax.ShapeDtypeStruct((vocab, width), F32),
        ),
        in_specs=[pl.BlockSpec(memory_space=pltpu.HBM)] * 6,
        out_specs=(vmem,) * 5,
        scratch_shapes=[
            pltpu.VMEM((rows, width), BF16),
            pltpu.VMEM((1, rows), jnp.int32),
            pltpu.VMEM((vocab, width), F32),
            pltpu.VMEM((taps, units), F32),
            pltpu.VMEM((rows, units), BF16),
            pltpu.VMEM((blocks, depth, units), BF16),
            pltpu.VMEM((2, total, width), BF16),
            pltpu.VMEM((2, EDGE, width), BF16),
            pltpu.VMEM((2, total, units), BF16),
            pltpu.VMEM((2, EDGE, units), BF16),
            pltpu.VMEM((width, 2 * rows), BF16),
            pltpu.VMEM((2 * depth, 2 * rows), BF16),
            pltpu.VMEM((2, total, units), F32),
            pltpu.VMEM((2, rows + 16, 128), F32),
            pltpu.VMEM((2, rows + 16, 128), F32),
            pltpu.VMEM((rows, units), F32),
            pltpu.VMEM((rows, units), BF16),
            pltpu.VMEM((CHUNKS, 2 * rows, cw), BF16),
            pltpu.VMEM((CHUNKS, 2 * rows, cw), BF16),
            pltpu.VMEM((rows, width), F32),
            pltpu.VMEM((rows, width), F32),
            pltpu.VMEM((CHUNKS, depth, cw), F32),
            pltpu.VMEM((CHUNKS, depth, cw), BF16),
            pltpu.VMEM((CHUNKS, depth, cw), BF16),
            pltpu.VMEM((CHUNKS, stacked_rows, cw), BF16),
            pltpu.VMEM((CHUNKS, stacked_rows, cw), BF16),
            pltpu.VMEM((CHUNKS, depth, cw), BF16),
            pltpu.VMEM((4, 24, units // 2), F32),
            pltpu.VMEM((bits + 2, 24, units // 2), F32),
            pltpu.VMEM((2, 24, units // 2), F32),
            dma((6,)),
            dma((4 * PIECES + 1,)), dma((4 * PIECES + 1,)),
            dma((5,)), dma((5,)),
            dma((CHUNKS, 2 + 2 * copies)), dma((CHUNKS, 2 + 2 * copies)),
            dma((bits + 3,)), dma((bits + 3,)),
        ],
        compiler_params=pltpu.CompilerParams(
            collective_id=0, has_side_effects=True, vmem_limit_bytes=60 * 1024 * 1024
        ),
        cost_estimate=pl.CostEstimate(
            flops=12 * rows * width * units, bytes_accessed=8 * rows * width, transcendentals=4 * rows * units
        ),
    )(
        window,
        token_codes.reshape(1, rows),
        embedding,
        weight,
        kernel,
        upstream,
    )
    block_result, grad_hidden, grad_weight, kernel_sum, table = pl.pallas_call(
        functools.partial(finish, factor),
        out_shape=(
            jax.ShapeDtypeStruct((rows, units), BF16),
            jax.ShapeDtypeStruct((rows, width), BF16),
            jax.ShapeDtypeStruct((depth, units), F32),
            jax.ShapeDtypeStruct((taps, units), F32),
            jax.ShapeDtypeStruct((vocab, width), F32),
        ),
        in_specs=[pl.BlockSpec(memory_space=pltpu.HBM)] * 5,
        out_specs=(pl.BlockSpec(memory_space=pltpu.HBM),) * 5,
        scratch_shapes=[pltpu.VMEM((depth, units), BF16), pltpu.VMEM((depth, units), F32), dma((12,))],
        compiler_params=pltpu.CompilerParams(vmem_limit_bytes=60 * 1024 * 1024),
    )(block_result, grad_hidden, grad_weight, kernel_sum, table)
    return (
        block_result[None],
        grad_hidden[None],
        grad_weight,
        kernel_sum,
        table,
    )


def solution(mesh):
    in_specs = (P("dp", "seq", None), P("dp", "seq"), P(), P("dp", None), P(), P("dp", "seq", None))
    out_specs = (P("dp", "seq", None), P("dp", "seq", None), P("dp", None), P(), P())
    return jax.shard_map(
        functools.partial(local, mesh.shape["seq"]),
        mesh=mesh, in_specs=in_specs, out_specs=out_specs, check_vma=False,
    )
```

profile of v0, /device:TPU:0, one launch (start us, length us, event | category | flops | bytes accessed | tf_op | source)
XLA Modules:
  0.0 115.7 jit_solution(16044921562551845290)
XLA Ops:
  0.6 87.0 %shard_map.101 = (bf16[128,1024]{1,0:T(8,128)(2,1)}, bf16[128,2048]{1,0:T(8,128)(2,1)}, bf16[512,1024]{1,0:T(8,128)(2,1)}, f32[7,1024]{1,0:T(8,128)}, f32[5,2048]{1,0:T(8,128)}) custom-call(bf16[128,2048]{1,0:T(8,128)(2,1)} %bitcast.4, s32[1,128]{1,0:T(1,128)} %tok_in.1, f32[5,2048]{1,0:T(8,128)} %emb_in.1, bf16[512,1024]{1,0:T(8,128)(2,1)} %w_in.1, ...), custom_call_target="tpu_custom_call" | custom-call | flops 3221225472 | bytes 2097152 | tf_op jit(solution)/shard_map/pallas_call | solution.py:551
  87.6 28.0 %shard_map.102 = (bf16[128,1024]{1,0:T(8,128)(2,1)}, bf16[128,2048]{1,0:T(8,128)(2,1)}, f32[512,1024]{1,0:T(8,128)}, f32[7,1024]{1,0:T(8,128)}, f32[5,2048]{1,0:T(8,128)}) custom-call(bf16[128,1024]{1,0:T(8,128)(2,1)} %get-tuple-element.15.b_in, bf16[128,2048]{1,0:T(8,128)(2,1)} %get-tuple-element.16.h_in, bf16[512,1024]{1,0:T(8,128)(2,1)} %get-tuple-element.17.g_in, ...), custom_call_target="tpu_custom_call" | custom-call | tf_op jit(solution)/shard_map/pallas_call | solution.py:613
where the time goes:
time: 116 us
  Pallas kernels  115 us (99%)
    pallas_call x1, Pallas kernels, local(): pl.pallas_call(functools.partial(body, seq_count, bits, factor), out_shap...  87 us
    pallas_call x1, Pallas kernels, local(): pl.pallas_call(functools.partial(finish, factor), out_shape=(jax.ShapeDty...  28 us

commit v1 on v0

--- a/solution.py
+++ b/solution.py
@@ -13,7 +13,6 @@
 BF16 = jnp.bfloat16
 EDGE = 16
 CHUNKS = 4
-PIECES = 4
 LANES = 256
 
 
@@ -51,13 +50,17 @@
     dp = lax.axis_index("dp")
     seq = lax.axis_index("seq")
     xi, ci = dp // 2, dp % 2
+    cw = units // CHUNKS
+    w_loads = [
+        pltpu.make_async_copy(w_in.at[:, pl.ds(p * cw, cw)], wg.at[p, dp], in_sems.at[5 + p]) for p in range(CHUNKS)
+    ]
     loads = [
         pltpu.make_async_copy(src, dst, in_sems.at[n])
         for n, (src, dst) in enumerate(
-            [(w_in, wg.at[dp]), (cot_in, cot_ref), (hid_in, hid_ref), (tok_in, tok_ref), (emb_in, emb_ref), (ker_in, ker_ref)]
+            [(cot_in, cot_ref), (hid_in, hid_ref), (tok_in, tok_ref), (emb_in, emb_ref), (ker_in, ker_ref)]
         )
     ]
-    for copy in loads:
+    for copy in w_loads + loads:
         copy.start()
     core_id = (dp + 1 - 2 * ci, seq)
     x_id = (dp + 2 - 4 * xi, seq)
@@ -98,23 +101,25 @@
     y_id = bit_ids[0]
     dpx = dp + 2 - 4 * xi
     half = depth // 2
-    piece = half // PIECES
-
-    def span(side, p):
-        return pl.ds(pl.multiple_of(side * half + p * piece, 16), piece)
-
-    sends = []
-    over_x = [
-        remote(wg.at[dp, span(yi, p)], wg.at[dp, span(yi, p)], w_ss.at[p], w_rs.at[p], x_id)
-        for p in range(PIECES)
-    ]
+
+    def part_of(p, block, side):
+        return wg.at[p, block, pl.ds(pl.multiple_of(side * half, 16), half)]
+
+    def passed(p, block, side, sem, who):
+        part = wg.at[p, block] if side is None else part_of(p, block, side)
+        return remote(part, part, w_ss.at[sem * CHUNKS + p], w_rs.at[sem * CHUNKS + p], who)
+
+    over_x = [passed(p, dp, yi, 0, x_id) for p in range(CHUNKS)]
+    own = [passed(p, dp, None, 1, core_id) for p in range(CHUNKS)]
+    over_y = [passed(p, dpx, yi, 2, y_id) for p in range(CHUNKS)]
+    over_core = [passed(p, dpx, yi, 3, core_id) for p in range(CHUNKS)]
+    over_core2 = [passed(p, dpx, 1 - yi, 4, core_id) for p in range(CHUNKS)]
+    for p in range(CHUNKS):
+        w_loads[p].wait()
+        over_x[p].start()
+        own[p].start()
     loads[0].wait()
-    for copy in over_x[:2]:
-        copy.start()
-    loads[1].wait()
-    own = remote(wg.at[dp], wg.at[dp], w_ss.at[4 * PIECES], w_rs.at[4 * PIECES], core_id)
-    own.start()
-    sends += over_x + [own]
+    sends = over_x + own + over_y + over_core + over_core2
     halo_u = [
         remote(cot_ref.at[pl.ds(rows - EDGE, EDGE)], hu.at[0], h_ss.at[0], h_rs.at[0], right_id),
         remote(cot_ref.at[pl.ds(0, EDGE)], hu.at[1], h_ss.at[1], h_rs.at[1], left_id),
@@ -123,7 +128,7 @@
         copy.start()
 
     tile = LANES
-    for copy in loads[2:]:
+    for copy in loads[1:]:
         copy.wait()
     tok = jnp.broadcast_to(tok_ref[...], (rows, rows)).astype(F32).T
     tok = jnp.concatenate([tok] * (tile // rows), axis=1) if tile > rows else tok[:, :tile]
@@ -145,22 +150,9 @@
         copy.start()
     sends += halo_u + halo_s
 
-    over_y, over_core = [], []
-
-    def arrived(p):
-        over_x[p].wait_recv()
-        if p + 2 < PIECES:
-            over_x[p + 2].start()
-        part = wg.at[dpx, span(yi, p)]
-        over_y.append(remote(part, part, w_ss.at[PIECES + p], w_rs.at[PIECES + p], y_id))
-        over_core.append(remote(part, part, w_ss.at[2 * PIECES + p], w_rs.at[2 * PIECES + p], core_id))
-        over_y[p].start()
-        over_core[p].start()
-
     has_left = (seq > 0).astype(F32)
     has_right = (seq < seq_count - 1).astype(F32)
     ux[0, pl.ds(EDGE, rows), :] = cot_ref[...]
-    arrived(0)
     for copy in halo_u + halo_s:
         copy.wait_recv()
     sx[0, pl.ds(0, EDGE), :] = (hx[0].astype(F32) * has_left).astype(BF16)
@@ -168,8 +160,6 @@
     ux[0, pl.ds(0, EDGE), :] = (hu[0].astype(F32) * has_left).astype(BF16)
     ux[0, pl.ds(rows + EDGE, EDGE), :] = (hu[1].astype(F32) * has_right).astype(BF16)
 
-    arrived(1)
-
     flip = (
         lax.broadcasted_iota(jnp.int32, (tile, tile), 0)
         + lax.broadcasted_iota(jnp.int32, (tile, tile), 1)
@@ -195,26 +185,16 @@
 
     lax.fori_loop(0, units // tile, reverse_up, 0)
 
-    def project(block, first):
-        depth_cols = pl.ds(pl.multiple_of(block * depth, depth), depth)
-
-        def project_tile(i, carry):
-            cols = pl.ds(pl.multiple_of(i * tile, tile), tile)
-            for s in range(2):
-                part = jnp.dot(sx[s, :, depth_cols], wg[block, :, cols], preferred_element_type=F32)
-                if first:
-                    val[s, :, cols] = part
-                else:
-                    val[s, :, cols] += part
-            return carry
-
-        lax.fori_loop(0, units // tile, project_tile, 0)
-
-    project(dp, True)
-
-    arrived(2)
-    own.wait_recv()
-    project(dp + 1 - 2 * ci, False)
+    def arrived_x(p):
+        over_x[p].wait_recv()
+        over_y[p].start()
+        over_core[p].start()
+        if p == CHUNKS - 1:
+            stream_copy.start()
+
+    def arrived_y(p):
+        over_y[p].wait_recv()
+        over_core2[p].start()
 
     def transpose_tile(i, carry):
         cols = pl.ds(pl.multiple_of(i * tile, tile), tile)
@@ -223,28 +203,12 @@
         return carry
 
     lax.fori_loop(0, width // tile, transpose_tile, 0)
-    for p in range(3, PIECES):
-        arrived(p)
     stream_copy = remote(
         s2t.at[pl.ds(pl.multiple_of((1 - xi) * 2 * depth, depth), 2 * depth)], s2tp, h_ss.at[4], h_rs.at[4], x_id
     )
-    stream_copy.start()
     sends.append(stream_copy)
-    over_core2 = []
-    for p in range(PIECES):
-        over_y[p].wait_recv()
-        other = 1 - yi
-        over_core2.append(
-            remote(wg.at[dpx, span(other, p)], wg.at[dpx, span(other, p)], w_ss.at[3 * PIECES + p], w_rs.at[3 * PIECES + p], core_id)
-        )
-        over_core2[p].start()
-    sends += over_y + over_core + over_core2
-    for p in range(PIECES):
-        over_core[p].wait_recv()
-        over_core2[p].wait_recv()
 
     ew = 128
-    cw = units // CHUNKS
     lo = EDGE - 8
 
     rt = 32
@@ -293,11 +257,18 @@
         return carry
 
     def elementwise(j):
-        cols = pl.ds(j * cw, cw)
-        for block in (dpx, dpx + 1 - 2 * ci):
-            depth_cols = pl.ds(pl.multiple_of(block * depth, depth), depth)
-            for s in range(2):
-                val[s, :, cols] += jnp.dot(sx[s, :, depth_cols], wg[block, :, cols], preferred_element_type=F32)
+        if j == 0:
+            arrived_x(0)
+        if j + 1 < CHUNKS:
+            arrived_x(j + 1)
+        arrived_y(j)
+        for copy in (own[j], over_core[j], over_core2[j]):
+            copy.wait_recv()
+        projected = jnp.zeros((2 * total, cw), F32)
+        for block in range(wg.shape[1]):
+            columns = sx[:, :, pl.ds(block * depth, depth)].reshape(2 * total, depth)
+            projected = projected + jnp.dot(columns, wg[j, block], preferred_element_type=F32)
+        val[:, :, pl.ds(j * cw, cw)] = projected.reshape(2, total, cw)
         lax.fori_loop(j * (cw // ew), (j + 1) * (cw // ew), strand_tile, 0)
         grad_copy(j).start()
 
@@ -392,7 +363,7 @@
             else:
                 gw_ref[:, pl.ds(j * cw, cw)] = gathered[j]
 
-        steps = [functools.partial(stage, j) for stage in (elementwise, product, after_core)]
+        steps = [functools.partial(stage, j) for stage in (product, after_core)]
         steps += [functools.partial(after_rs, b) for b in range(len(levels))]
         steps += [functools.partial(after_ag, n) for n in range(len(gathers))]
         return steps
@@ -405,7 +376,7 @@
         part = jnp.zeros((2 * rows, tile), F32)
         for j in range(CHUNKS):
             part = part + lax.dot_general(
-                gv[j], wg[b, r, pl.ds(j * cw, cw)], (((1,), (1,)), ((), ())), preferred_element_type=F32
+                gv[j], wg[j, b, r, :], (((1,), (1,)), ((), ())), preferred_element_type=F32
             )
         fwd_back[:, cols] = part[:rows]
         rev_back[:, mirror] = mirrored(part[rows:].astype(BF16))
@@ -474,19 +445,19 @@
         lax.fori_loop(0, units // tile, result_tile, 0)
         small_step(0)
 
-    fillers = [functools.partial(fill_back, part) for part in range(4)] + [fill_input, fill_result]
-    fillers += [functools.partial(small_step, n) for n in range(1, bits + 2)]
-
+    for j in range(CHUNKS):
+        elementwise(j)
+    for part in range(4):
+        fill_back(part)
+    fillers = [fill_input, fill_result] + [functools.partial(small_step, n) for n in range(1, bits + 2)]
     plans = [stages(j) for j in range(CHUNKS)]
     length = len(plans[0])
     for wave in range(length + CHUNKS - 1):
-        if wave < CHUNKS:
-            plans[wave][0]()
         for j in range(CHUNKS):
-            if 1 <= wave - j < length:
+            if 0 <= wave - j < length:
                 plans[j][wave - j]()
-                if wave >= CHUNKS and fillers:
-                    fillers.pop(0)()
+        if fillers:
+            fillers.pop(0)()
     for filler in fillers:
         filler()
     small_last().wait_recv()
@@ -511,24 +482,23 @@
     small_last().wait_send()
 
 
-def finish(factor, b_in, h_in, g_in, k_in, t_in, b_out, h_out, g_out, k_out, t_out, narrow, wide, sems):
-    copies = [
-        pltpu.make_async_copy(src, dst, sems.at[n])
-        for n, (src, dst) in enumerate([(h_in, h_out), (b_in, b_out), (k_in, k_out), (t_in, t_out)])
-    ]
+def finish(factor, b_in, h_in, g_in, k_in, t_in, b_out, h_out, g_out, k_out, t_out, b_mid, h_mid, k_mid, t_mid, narrow, wide, sems):
     step = g_in.shape[0] // 4
     parts = [pl.ds(q * step, step) for q in range(4)]
-    fetches = [pltpu.make_async_copy(g_in.at[part], narrow.at[part], sems.at[8 + q]) for q, part in enumerate(parts)]
+    inward = [(g_in.at[part], narrow.at[part]) for part in parts]
+    inward += [(h_in, h_mid), (b_in, b_mid), (t_in, t_mid), (k_in, k_mid)]
+    outward = [(wide.at[part], g_out.at[part]) for part in parts]
+    outward += [(h_mid, h_out), (b_mid, b_out), (t_mid, t_out), (k_mid, k_out)]
+    fetches = [pltpu.make_async_copy(src, dst, sems.at[n]) for n, (src, dst) in enumerate(inward)]
+    stores = [pltpu.make_async_copy(src, dst, sems.at[8 + n]) for n, (src, dst) in enumerate(outward)]
     for copy in fetches:
         copy.start()
-    for copy in copies:
-        copy.start()
-    for q, part in enumerate(parts):
-        fetches[q].wait()
-        wide[part, :] = narrow[part, :].astype(F32) * factor
-        copies.append(pltpu.make_async_copy(wide.at[part], g_out.at[part], sems.at[4 + q]))
-        copies[-1].start()
-    for copy in copies:
+    for n in range(8):
+        fetches[n].wait()
+        if n < 4:
+            wide[parts[n], :] = narrow[parts[n], :].astype(F32) * factor
+        stores[n].start()
+    for copy in stores:
         copy.wait()
 
 
@@ -565,7 +535,7 @@
             pltpu.VMEM((vocab, width), F32),
             pltpu.VMEM((taps, units), F32),
             pltpu.VMEM((rows, units), BF16),
-            pltpu.VMEM((blocks, depth, units), BF16),
+            pltpu.VMEM((CHUNKS, blocks, depth, cw), BF16),
             pltpu.VMEM((2, total, width), BF16),
             pltpu.VMEM((2, EDGE, width), BF16),
             pltpu.VMEM((2, total, units), BF16),
@@ -590,8 +560,8 @@
             pltpu.VMEM((4, 24, units // 2), F32),
             pltpu.VMEM((bits + 2, 24, units // 2), F32),
             pltpu.VMEM((2, 24, units // 2), F32),
-            dma((6,)),
-            dma((4 * PIECES + 1,)), dma((4 * PIECES + 1,)),
+            dma((5 + CHUNKS,)),
+            dma((5 * CHUNKS,)), dma((5 * CHUNKS,)),
             dma((5,)), dma((5,)),
             dma((CHUNKS, 2 + 2 * copies)), dma((CHUNKS, 2 + 2 * copies)),
             dma((bits + 3,)), dma((bits + 3,)),
@@ -621,7 +591,15 @@
         ),
         in_specs=[pl.BlockSpec(memory_space=pltpu.HBM)] * 5,
         out_specs=(pl.BlockSpec(memory_space=pltpu.HBM),) * 5,
-        scratch_shapes=[pltpu.VMEM((depth, units), BF16), pltpu.VMEM((depth, units), F32), dma((12,))],
+        scratch_shapes=[
+            pltpu.VMEM((rows, units), BF16),
+            pltpu.VMEM((rows, width), BF16),
+            pltpu.VMEM((taps, units), F32),
+            pltpu.VMEM((vocab, width), F32),
+            pltpu.VMEM((depth, units), BF16),
+            pltpu.VMEM((depth, units), F32),
+            dma((16,)),
+        ],
         compiler_params=pltpu.CompilerParams(vmem_limit_bytes=60 * 1024 * 1024),
     )(block_result, grad_hidden, grad_weight, kernel_sum, table)
     return (

time: 116 us -> 89.9 us (0.78)
  Pallas kernels: 115 us -> 89.1 us
    pallas_call x1, Pallas kernels: 28 us -> 2.71 us  [local(): pl.pallas_call(functools.partial(finish, factor), out_shape=(jax.ShapeDty...]
where the time goes in v1:
time: 89.9 us; the launch traced here: 89.8 us
  Pallas kernels  89.1 us (99%)
    pallas_call x1, Pallas kernels, local(): pl.pallas_call(functools.partial(body, seq_count, bits, factor), out_shap...  86.4 us
    pallas_call x1, Pallas kernels, local(): pl.pallas_call(functools.partial(finish, factor), out_shape=(jax.ShapeDty...  2.71 us

profile of v1, /device:TPU:0, one launch (start us, length us, event | category | flops | bytes accessed | tf_op | source)
XLA Modules:
  0.0 89.8 jit_solution(15825472044984727350)
XLA Ops:
  0.6 86.4 %shard_map.101 = (bf16[128,1024]{1,0:T(8,128)(2,1)}, bf16[128,2048]{1,0:T(8,128)(2,1)}, bf16[512,1024]{1,0:T(8,128)(2,1)}, f32[7,1024]{1,0:T(8,128)}, f32[5,2048]{1,0:T(8,128)}) custom-call(bf16[128,2048]{1,0:T(8,128)(2,1)} %bitcast.4, s32[1,128]{1,0:T(1,128)} %tok_in.1, f32[5,2048]{1,0:T(8,128)} %emb_in.1, bf16[512,1024]{1,0:T(8,128)(2,1)} %w_in.1, ...), custom_call_target="tpu_custom_call" | custom-call | flops 3221225472 | bytes 2097152 | tf_op jit(solution)/shard_map/pallas_call | solution.py:521
  87.0 2.7 %shard_map.102 = (bf16[128,1024]{1,0:T(8,128)(2,1)}, bf16[128,2048]{1,0:T(8,128)(2,1)}, f32[512,1024]{1,0:T(8,128)}, f32[7,1024]{1,0:T(8,128)}, f32[5,2048]{1,0:T(8,128)}) custom-call(bf16[128,1024]{1,0:T(8,128)(2,1)} %get-tuple-element.15.b_in, bf16[128,2048]{1,0:T(8,128)(2,1)} %get-tuple-element.16.h_in, bf16[512,1024]{1,0:T(8,128)(2,1)} %get-tuple-element.17.g_in, ...), custom_call_target="tpu_custom_call" | custom-call | tf_op jit(solution)/shard_map/pallas_call | solution.py:583
